TPU v7x, 32 devices: a whole 2x2x4 slice. The times are simulated.
32 devices in a mesh: dp: 2 (over x), expert: 4 (over y, core), mp: 4 (over z).
Axes of the slice: x: 2, y: 2, z: 4, core: 2. Of those that a mesh axis runs over, the one named last changes fastest.
Arguments:
- tokens: bfloat16 [128, 3072], P('dp'), may hold values from -6 to 6
- expert_ids: int32 [128, 2], P('dp'), may hold values from 0 to 3, all different within a row; in each aligned block of 64 rows (0 to 63, 64 to 127, ...) at most 64 rows name the same one
- gate_values: float32 [128, 2], P('dp'), may hold values from 0.2 to 1
- targets: int32 [128], P('dp'), may hold values from 0 to 32767
- w_gate: bfloat16 [4, 3072, 4, 2048], P('expert', None, 'mp', 'dp'), may hold values from -0.109375 to 0.109375
- w_up: bfloat16 [4, 3072, 4, 2048], P('expert', None, 'mp', 'dp'), may hold values from -0.109375 to 0.109375
- w_down: bfloat16 [4, 4, 2048, 3072], P('expert', 'mp', None, 'dp'), may hold values from -0.0625 to 0.0625
- norm_gain: float32 [3072], replicated, may hold values from 0.1 to 1.9
- lens_head: bfloat16 [3072, 32768], P('dp', ('expert', 'mp')), may hold values from -120 to 120
Outputs:
- mixed: bfloat16 [128, 3072], P('dp')
- log_probs: float32 [128], P('dp')
Inputs may be any that keep to these rules, and one draw needn't show every extreme that they name: `expert_ids`: each row names two different experts; in each aligned block of 64 rows no expert is named by more than 64 rows, a bound that some block reaches.
All inputs are finite; a program needn't handle non-finite values.
Results may differ from a plain program's by a relative error of at most 0.0041.
Values may be sent and summed in bfloat16 or wider, within the bound.
A program may use at most 128 MiB of HBM per device.

v0:
```python
import jax
import jax.numpy as jnp
from jax import lax
from jax.sharding import PartitionSpec as P

f32, bf16 = (jnp.float32, jnp.bfloat16)


def per_device(
    tokens, expert_ids, gate_values, targets, w_gate, w_up, w_down, norm_gain, lens_head
):
    rows, feats = tokens.shape
    owner = lax.axis_index("expert")
    weights = jnp.sum(jnp.where(expert_ids == owner, gate_values, f32(0.0)), axis=1)
    gate_mat = w_gate.reshape(feats, -1)
    up_mat = w_up.reshape(feats, -1)
    down_mat = w_down.reshape(w_down.shape[2], w_down.shape[3])
    own_feats = down_mat.shape[1]
    all_tokens = lax.all_gather(tokens, "dp", axis=0, tiled=True)
    all_weights = lax.all_gather(weights, "dp", axis=0, tiled=True)
    gate_part = jnp.dot(all_tokens, gate_mat, preferred_element_type=f32)
    up_part = jnp.dot(all_tokens, up_mat, preferred_element_type=f32)
    hidden = (jax.nn.silu(gate_part) * up_part).astype(bf16)
    hidden = lax.all_gather(hidden, "dp", axis=1, tiled=True)
    part = jnp.dot(hidden, down_mat, preferred_element_type=f32) * all_weights[:, None]
    summed = lax.psum(part, ("expert", "mp"))
    first = lax.axis_index("dp") * own_feats
    own_tokens = lax.dynamic_slice_in_dim(all_tokens, first, own_feats, axis=1)
    own_gain = lax.dynamic_slice_in_dim(norm_gain, first, own_feats, axis=0)
    mixed_part = (own_tokens.astype(f32) + summed).astype(bf16)
    mixed = lax.all_to_all(mixed_part, "dp", split_axis=0, concat_axis=1, tiled=True)
    mixed_f = mixed.astype(f32)
    scale = lax.rsqrt(jnp.mean(mixed_f * mixed_f, axis=1) + 1e-05)
    gained = (mixed_part.astype(f32) * own_gain[None, :]).astype(bf16)
    logits_part = jnp.dot(gained, lens_head, preferred_element_type=f32)
    logits = lax.psum_scatter(logits_part, "dp", scatter_dimension=0, tiled=True)
    logits = logits * scale[:, None]
    vocab_cols = lens_head.shape[1]
    vocab_start = (owner * lax.axis_size("mp") + lax.axis_index("mp")) * vocab_cols
    columns = vocab_start + lax.broadcasted_iota(jnp.int32, (1, vocab_cols), 1)
    hit = columns == targets[:, None]
    target_local = jnp.sum(jnp.where(hit, logits, f32(0.0)), axis=1)
    top = jnp.max(logits, axis=1)
    total = jnp.sum(jnp.exp(logits - top[:, None]), axis=1)
    stats = lax.all_gather(jnp.stack([top, total, target_local]), ("expert", "mp"))
    tops, totals, hits = (stats[:, 0], stats[:, 1], stats[:, 2])
    top_all = jnp.max(tops, axis=0)
    exp_total = jnp.sum(totals * jnp.exp(tops - top_all[None, :]), axis=0)
    log_probs = jnp.sum(hits, axis=0) - top_all - jnp.log(exp_total)
    return (mixed, log_probs)


def solution(mesh):
    in_specs = (
        P("dp", None),
        P("dp", None),
        P("dp", None),
        P("dp"),
        P("expert", None, "mp", "dp"),
        P("expert", None, "mp", "dp"),
        P("expert", "mp", None, "dp"),
        P(),
        P("dp", ("expert", "mp")),
    )
    out_specs = (P("dp", None), P("dp"))
    return jax.shard_map(
        per_device, mesh=mesh, in_specs=in_specs, out_specs=out_specs, check_vma=False
    )
```

profile of v0, /device:TPU:0, one launch (start us, length us, event | category | flops | bytes accessed | tf_op | source)
XLA Modules:
  0.0 207.5 jit_solution(1650163457520954662)
XLA Ops:
  7.2 0.0 all-reduce.3.cloned.1.call-start
  7.2 0.0 slice-start
  7.2 13.1 %all_gather.15 = bf16[128,3072]{1,0:T(8,128)(2,1)S(1)} all-gather(bf16[64,3072]{1,0:T(8,128)(2,1)} %param.9), channel_id=1, replica_groups=mesh['dp'=2,'expert'=4,'mp'=4] {'dp'}, dimensions={0}, use_global_device_ids=true | all-gather | bytes 1179648 | tf_op jit(solution)/shard_map/all_gather | solution.py:19
  20.3 3.9 %fusion.4 = f32[128,1024]{1,0:T(8,128)S(1)} fusion(bf16[128,3072]{1,0:T(8,128)(2,1)S(1)} %all_gather.15, bf16[1,3072,1,1024]{3,1,2,0:T(8,128)(2,1)} %param.13), kind=kOutput, calls=%fused_computation.4 | convolution fusion | flops 805306368 | bytes 7602176 | tf_op jit(solution)/shard_map/dot_general | solution.py:21
  24.2 0.0 slice-done
  24.2 0.0 slice-done.1
  24.3 0.0 copy-start.4
  24.3 0.0 copy-start.1
  24.3 0.0 copy-start.2
  24.3 1.1 fusion.12
  25.4 8.2 %all_gather.16 = bf16[128,2048]{1,0:T(8,128)(2,1)S(1)} all-gather(bf16[128,1024]{1,0:T(8,128)(2,1)S(1)} %fusion.12), channel_id=1, replica_groups=mesh['dp'=2,'expert'=4,'mp'=4] {'dp'}, dimensions={1}, use_global_device_ids=true | all-gather | bytes 786432 | tf_op jit(solution)/shard_map/all_gather | solution.py:24
  33.6 0.0 copy-done.4
  33.6 0.6 dynamic-slice
  34.9 0.2 dynamic-update-slice
  35.1 4.9 %all-reduce = f32[128]{0:T(128)S(1)} all-reduce(f32[128]{0:T(128)S(1)} %dynamic-update-slice), channel_id=1, replica_groups=mesh['dp'=2,'expert'=4,'mp'=4] {'dp'}, use_global_device_ids=true, to_apply=%add | all-reduce | flops 128 | bytes 1024
  40.0 4.7 %fusion.6 = f32[128,1536]{1,0:T(8,128)} fusion(bf16[128,2048]{1,0:T(8,128)(2,1)S(1)} %all_gather.16, bf16[1,1,2048,1536]{3,2,1,0:T(8,128)(2,1)} %param.15, f32[128]{0:T(128)S(1)} %all-reduce), kind=kOutput, calls=%fused_computation.6 | convolution fusion | flops 805502976 | bytes 7602688 | tf_op jit(solution)/shard_map/dot_general | solution.py:25
  44.7 0.0 all-reduce.3.cloned.1.call-update
  44.7 0.0 reduce-scatter.2.cloned.1.call-start
  44.8 0.1 dynamic_slice.7
  44.9 93.2 %all-reduce.3.cloned.1.call-done = f32[128,1536]{1,0:T(8,128)} async-done(((f32[128,1536]{1,0:T(8,128)}), f32[128,1536]{1,0:T(8,128)}) %all-reduce.3.cloned.1.call-update) | async-done | bytes 786448 | tf_op jit(solution)/shard_map/psum | solution.py:26
  138.1 1.9 add_convert_fusion
  140.0 4.9 %fusion.15 = f32[128,2048]{1,0:T(8,128)} fusion(bf16[1536,2048]{1,0:T(8,128)(2,1)} %param.17, bf16[128,1536]{1,0:T(8,128)(2,1)} %add_convert_fusion, f32[1536]{0:T(1024)S(1)} %dynamic_slice.7), kind=kOutput, calls=%fused_computation.15 | convolution fusion | flops 805896192 | bytes 7739392 | tf_op jit(solution)/shard_map/dot_general | solution.py:35
  144.9 0.0 reduce-scatter.2.cloned.1.call-update
  145.0 3.5 %all-to-all-start = ((bf16[2,64,1536]{2,1,0:T(8,128)(2,1)}), bf16[2,64,1536]{2,1,0:T(8,128)(2,1)S(1)}, u32[]{:S(2)}, u32[]{:S(2)}) async-start(bf16[2,64,1536]{2,1,0:T(8,128)(2,1)} %bitcast.4), calls=%async_computation | async-start | bytes 786432 | tf_op jit(solution)/shard_map/all_to_all | solution.py:31
  148.5 10.2 %all-to-all-done = bf16[2,64,1536]{2,1,0:T(8,128)(2,1)S(1)} async-done(((bf16[2,64,1536]{2,1,0:T(8,128)(2,1)}), bf16[2,64,1536]{2,1,0:T(8,128)(2,1)S(1)}, u32[]{:S(2)}, u32[]{:S(2)}) %all-to-all-start) | async-done | bytes 393248 | tf_op jit(solution)/shard_map/all_to_all | solution.py:31
  158.6 0.8 copy.16
  159.4 0.2 multiply_reduce_fusion
  159.6 7.2 %reduce-scatter.2.cloned.1.call-done = f32[64,2048]{1,0:T(8,128)} async-done(((f32[128,2048]{1,0:T(8,128)}), f32[64,2048]{1,0:T(8,128)}) %reduce-scatter.2.cloned.1.call-update) | async-done | bytes 524304 | tf_op jit(solution)/shard_map/reduce_scatter | solution.py:36
  166.8 1.2 multiply_reduce_fusion.1
  168.0 1.4 exponential_reduce_fusion
  169.4 30.6 %all-gather.1 = f32[16,3,64]{2,1,0:T(4,128)S(1)} all-gather(f32[1,3,64]{2,1,0:T(4,128)S(1)} %maximum_bitcast_fusion), channel_id=2, replica_groups=mesh['dp'=2,'expert'=4,'mp'=4] {'expert','mp'}, dimensions={0}, use_global_device_ids=true | all-gather | bytes 13056 | tf_op jit(solution)/shard_map/all_gather | solution.py:45
  200.1 0.5 log_subtract_fusion
  (15 shorter events, 0.1 us)
Async XLA Ops:
  7.2 130.9 %all-reduce.3.cloned.1.call-start = ((), (), s32[]{:S(2)}) async-start(), calls=%async_computation.2 | async-start | bytes 1572864 | tf_op jit(solution)/shard_map/psum | solution.py:26
  7.2 17.0 %slice-start = ((s8[6291456]{0:T(1024)(128)(4,1)}), s8[4194304]{0:T(1024)(128)(4,1)S(1)}, s32[]{:S(2)}) async-start(s8[6291456]{0:T(1024)(128)(4,1)} %bitcast.41), calls=%async_computation.4 | async-start | bytes 8388608
  20.3 3.9 %slice-start.1 = ((s8[6291456]{0:T(1024)(128)(4,1)}), s8[2097152]{0:T(1024)(128)(4,1)S(1)}, s32[]{:S(2)}) async-start(s8[6291456]{0:T(1024)(128)(4,1)} %bitcast.41), calls=%async_computation.5 | async-start | bytes 4194304
  24.3 9.3 %copy-start.4 = (u32[32]{0:T(128)S(1)}, u32[32]{0:T(128)}, u32[]{:S(2)}) copy-start(u32[32]{0:T(128)} %constant.40) | copy-start | bytes 388
  24.3 10.5 %copy-start.1 = (f32[64,2]{0,1:T(2,128)S(1)}, f32[64,2]{0,1:T(2,128)}, u32[]{:S(2)}) copy-start(f32[64,2]{0,1:T(2,128)} %param.11) | copy-start | bytes 1540
  24.3 10.5 %copy-start.2 = (s32[64,2]{0,1:T(2,128)S(1)}, s32[64,2]{0,1:T(2,128)}, u32[]{:S(2)}) copy-start(s32[64,2]{0,1:T(2,128)} %param.10) | copy-start | bytes 1540
  40.0 4.8 %copy-start = (f32[3072]{0:T(1024)S(1)}, f32[3072]{0:T(1024)}, u32[]{:S(2)}) copy-start(f32[3072]{0:T(1024)} %param.16) | copy-start | bytes 36868
  44.7 122.0 %reduce-scatter.2.cloned.1.call-start = ((), (), s32[]{:S(2)}) async-start(), calls=%async_computation.3 | async-start | bytes 1572864 | tf_op jit(solution)/shard_map/reduce_scatter | solution.py:36
  44.9 123.1 %copy-start.3 = (s32[64]{0:T(128)S(1)}, s32[64]{0:T(128)}, u32[]{:S(2)}) copy-start(s32[64]{0:T(128)} %param.12) | copy-start | bytes 772
  145.0 13.7 %all-to-all-start = ((bf16[2,64,1536]{2,1,0:T(8,128)(2,1)}), bf16[2,64,1536]{2,1,0:T(8,128)(2,1)S(1)}, u32[]{:S(2)}, u32[]{:S(2)}) async-start(bf16[2,64,1536]{2,1,0:T(8,128)(2,1)} %bitcast.4), calls=%async_computation | async-start | bytes 786432 | tf_op jit(solution)/shard_map/all_to_all | solution.py:31
Sparse Core Ops, SparseCore 0:
  44.9 93.1 all-reduce.2
  145.1 21.6 reduce-scatter.1
where the time goes:
time: 208 us; the launch traced here: 207 us
  waiting for transfers between devices  111 us (53%)
  blocking collectives  56.8 us (27%)
  between operations  14.9 us (7%)
  matrix products  14.6 us (7%)
  other arithmetic  5.39 us (3%)
  starting transfers between devices  3.56 us (2%)
    psum x1, waiting for transfers between devices, per_device(): summed = lax.psum(part, ('expert', 'mp'))  93.2 us
    all_gather x1, blocking collectives, per_device(): lax.all_gather(jnp.stack([top, total, target_local]), ('expert', 'mp'))  30.6 us
    all_gather x1, blocking collectives, per_device(): all_tokens = lax.all_gather(tokens, 'dp', axis=0, tiled=True)  13.1 us
    all_to_all x1, waiting for transfers between devices, per_device(): lax.all_to_all(mixed_part, 'dp', split_axis=0, concat_axis=1, tiled=True)  10.2 us
    all_gather x1, blocking collectives, per_device(): hidden = lax.all_gather(hidden, 'dp', axis=1, tiled=True)  8.17 us
    reduce_scatter x1, waiting for transfers between devices, per_device(): lax.psum_scatter(logits_part, 'dp', scatter_dimension=0, tiled=True)  7.19 us
    unnamed x1, blocking collectives  4.92 us
    dot_general x1, matrix products, per_device(): logits_part = jnp.dot(gained, lens_head, preferred_element_type=f32)  4.91 us
  transfers between devices with their start and end apart: 3, of which 3 were waited for; matrix products, arithmetic and copies ran while one was open for 1% of the time, Pallas kernels for 0%

commit v1 on v0

--- a/solution.py
+++ b/solution.py
@@ -23,7 +23,9 @@
     hidden = (jax.nn.silu(gate_part) * up_part).astype(bf16)
     hidden = lax.all_gather(hidden, "dp", axis=1, tiled=True)
     part = jnp.dot(hidden, down_mat, preferred_element_type=f32) * all_weights[:, None]
-    summed = lax.psum(part, ("expert", "mp"))
+    summed = part
+    for over in ("mp", "expert"):
+        summed = lax.psum(summed, over)
     first = lax.axis_index("dp") * own_feats
     own_tokens = lax.dynamic_slice_in_dim(all_tokens, first, own_feats, axis=1)
     own_gain = lax.dynamic_slice_in_dim(norm_gain, first, own_feats, axis=0)

time: 208 us -> 197 us (0.947)
  waiting for transfers between devices: 111 us -> 98.4 us
    psum x1 -> x2, waiting for transfers between devices: 93.2 us -> 81.2 us  [per_device(): summed = lax.psum(summed, over)]
  transfers between devices with their start and end apart: 3 -> 4, of which waited for: 3 -> 4; matrix products, arithmetic and copies ran while one was open for 1% -> 1% of each run, Pallas kernels for 0% -> 0%
where the time goes in v1:
time: 197 us
  waiting for transfers between devices  98.4 us (50%)
  blocking collectives  58.4 us (30%)
  matrix products  14.6 us (7%)
  between operations  14.6 us (7%)
  other arithmetic  5.39 us (3%)
  starting transfers between devices  3.6 us (2%)
    psum x2, waiting for transfers between devices, per_device(): summed = lax.psum(summed, over)  81.2 us
    all_gather x1, blocking collectives, per_device(): lax.all_gather(jnp.stack([top, total, target_local]), ('expert', 'mp'))  32.2 us
    all_gather x1, blocking collectives, per_device(): all_tokens = lax.all_gather(tokens, 'dp', axis=0, tiled=True)  13.1 us
    reduce_scatter x1, waiting for transfers between devices, per_device(): lax.psum_scatter(logits_part, 'dp', scatter_dimension=0, tiled=True)  9.06 us
    all_to_all x1, waiting for transfers between devices, per_device(): lax.all_to_all(mixed_part, 'dp', split_axis=0, concat_axis=1, tiled=True)  8.18 us
    all_gather x1, blocking collectives, per_device(): hidden = lax.all_gather(hidden, 'dp', axis=1, tiled=True)  8.17 us
    unnamed x1, blocking collectives  4.92 us
    dot_general x1, matrix products, per_device(): logits_part = jnp.dot(gained, lens_head, preferred_element_type=f32)  4.91 us
  transfers between devices with their start and end apart: 4, of which 4 were waited for; matrix products, arithmetic and copies ran while one was open for 1% of the time, Pallas kernels for 0%

profile of v1, /device:TPU:0, one launch (start us, length us, event | category | flops | bytes accessed | tf_op | source)
XLA Modules:
  0.0 196.7 jit_solution(14776009412464102762)
XLA Ops:
  7.2 0.0 all-reduce.4.cloned.1.call-start
  7.2 0.0 slice-start
  7.2 13.1 %all_gather.15 = bf16[128,3072]{1,0:T(8,128)(2,1)S(1)} all-gather(bf16[64,3072]{1,0:T(8,128)(2,1)} %param.9), channel_id=1, replica_groups=mesh['dp'=2,'expert'=4,'mp'=4] {'dp'}, dimensions={0}, use_global_device_ids=true | all-gather | bytes 1179648 | tf_op jit(solution)/shard_map/all_gather | solution.py:19
  20.3 3.9 %fusion.4 = f32[128,1024]{1,0:T(8,128)S(1)} fusion(bf16[128,3072]{1,0:T(8,128)(2,1)S(1)} %all_gather.15, bf16[1,3072,1,1024]{3,1,2,0:T(8,128)(2,1)} %param.13), kind=kOutput, calls=%fused_computation.4 | convolution fusion | flops 805306368 | bytes 7602176 | tf_op jit(solution)/shard_map/dot_general | solution.py:21
  24.3 0.0 copy-start.4
  24.3 0.0 copy-start.1
  24.3 0.0 copy-start.2
  24.3 1.1 fusion.12
  25.4 8.2 %all_gather.16 = bf16[128,2048]{1,0:T(8,128)(2,1)S(1)} all-gather(bf16[128,1024]{1,0:T(8,128)(2,1)S(1)} %fusion.12), channel_id=1, replica_groups=mesh['dp'=2,'expert'=4,'mp'=4] {'dp'}, dimensions={1}, use_global_device_ids=true | all-gather | bytes 786432 | tf_op jit(solution)/shard_map/all_gather | solution.py:24
  33.6 0.6 dynamic-slice
  34.9 0.2 dynamic-update-slice
  35.1 4.9 %all-reduce = f32[128]{0:T(128)S(1)} all-reduce(f32[128]{0:T(128)S(1)} %dynamic-update-slice), channel_id=1, replica_groups=mesh['dp'=2,'expert'=4,'mp'=4] {'dp'}, use_global_device_ids=true, to_apply=%add | all-reduce | flops 128 | bytes 1024
  40.0 4.7 %fusion.6 = f32[128,1536]{1,0:T(8,128)} fusion(bf16[128,2048]{1,0:T(8,128)(2,1)S(1)} %all_gather.16, bf16[1,1,2048,1536]{3,2,1,0:T(8,128)(2,1)} %param.15, f32[128]{0:T(128)S(1)} %all-reduce), kind=kOutput, calls=%fused_computation.6 | convolution fusion | flops 805502976 | bytes 7602688 | tf_op jit(solution)/shard_map/dot_general | solution.py:25
  44.7 0.0 all-reduce.4.cloned.1.call-update
  44.7 0.0 all-reduce.6.cloned.1.call-start
  44.8 45.0 %all-reduce.4.cloned.1.call-done = f32[128,1536]{1,0:T(8,128)} async-done(((f32[128,1536]{1,0:T(8,128)}), f32[128,1536]{1,0:T(8,128)}) %all-reduce.4.cloned.1.call-update) | async-done | bytes 786448 | tf_op jit(solution)/shard_map/psum | solution.py:28
  89.7 0.0 all-reduce.6.cloned.1.call-update
  89.8 0.0 reduce-scatter.2.cloned.1.call-start
  89.8 0.1 dynamic_slice.7
  89.9 36.2 %all-reduce.6.cloned.1.call-done = f32[128,1536]{1,0:T(8,128)} async-done(((f32[128,1536]{1,0:T(8,128)}), f32[128,1536]{1,0:T(8,128)}) %all-reduce.6.cloned.1.call-update) | async-done | bytes 786448 | tf_op jit(solution)/shard_map/psum | solution.py:28
  126.1 1.9 add_convert_fusion
  128.1 4.9 %fusion.15 = f32[128,2048]{1,0:T(8,128)} fusion(bf16[1536,2048]{1,0:T(8,128)(2,1)} %param.17, bf16[128,1536]{1,0:T(8,128)(2,1)} %add_convert_fusion, f32[1536]{0:T(1024)S(1)} %dynamic_slice.7), kind=kOutput, calls=%fused_computation.15 | convolution fusion | flops 805896192 | bytes 7739392 | tf_op jit(solution)/shard_map/dot_general | solution.py:37
  133.0 0.0 reduce-scatter.2.cloned.1.call-update
  133.0 3.5 %all-to-all-start = ((bf16[2,64,1536]{2,1,0:T(8,128)(2,1)}), bf16[2,64,1536]{2,1,0:T(8,128)(2,1)S(1)}, u32[]{:S(2)}, u32[]{:S(2)}) async-start(bf16[2,64,1536]{2,1,0:T(8,128)(2,1)} %bitcast.4), calls=%async_computation | async-start | bytes 786432 | tf_op jit(solution)/shard_map/all_to_all | solution.py:33
  136.5 8.2 %all-to-all-done = bf16[2,64,1536]{2,1,0:T(8,128)(2,1)S(1)} async-done(((bf16[2,64,1536]{2,1,0:T(8,128)(2,1)}), bf16[2,64,1536]{2,1,0:T(8,128)(2,1)S(1)}, u32[]{:S(2)}, u32[]{:S(2)}) %all-to-all-start) | async-done | bytes 393248 | tf_op jit(solution)/shard_map/all_to_all | solution.py:33
  144.7 0.8 copy.16
  145.5 0.2 multiply_reduce_fusion
  145.6 9.1 %reduce-scatter.2.cloned.1.call-done = f32[64,2048]{1,0:T(8,128)} async-done(((f32[128,2048]{1,0:T(8,128)}), f32[64,2048]{1,0:T(8,128)}) %reduce-scatter.2.cloned.1.call-update) | async-done | bytes 524304 | tf_op jit(solution)/shard_map/reduce_scatter | solution.py:38
  154.7 1.2 multiply_reduce_fusion.1
  156.0 1.4 exponential_reduce_fusion
  157.4 32.2 %all-gather.1 = f32[16,3,64]{2,1,0:T(4,128)S(1)} all-gather(f32[1,3,64]{2,1,0:T(4,128)S(1)} %maximum_bitcast_fusion), channel_id=2, replica_groups=mesh['dp'=2,'expert'=4,'mp'=4] {'expert','mp'}, dimensions={0}, use_global_device_ids=true | all-gather | bytes 13056 | tf_op jit(solution)/shard_map/all_gather | solution.py:47
  189.6 0.5 log_subtract_fusion
  (18 shorter events, 0.1 us)
Async XLA Ops:
  7.2 82.6 %all-reduce.4.cloned.1.call-start = ((), (), s32[]{:S(2)}) async-start(), calls=%async_computation.2 | async-start | bytes 1572864 | tf_op jit(solution)/shard_map/psum | solution.py:28
  7.2 17.0 %slice-start = ((s8[6291456]{0:T(1024)(128)(4,1)}), s8[4194304]{0:T(1024)(128)(4,1)S(1)}, s32[]{:S(2)}) async-start(s8[6291456]{0:T(1024)(128)(4,1)} %bitcast.41), calls=%async_computation.5 | async-start | bytes 8388608
  20.3 3.9 %slice-start.1 = ((s8[6291456]{0:T(1024)(128)(4,1)}), s8[2097152]{0:T(1024)(128)(4,1)S(1)}, s32[]{:S(2)}) async-start(s8[6291456]{0:T(1024)(128)(4,1)} %bitcast.41), calls=%async_computation.6 | async-start | bytes 4194304
  24.3 9.3 %copy-start.4 = (u32[32]{0:T(128)S(1)}, u32[32]{0:T(128)}, u32[]{:S(2)}) copy-start(u32[32]{0:T(128)} %constant.40) | copy-start | bytes 388
  24.3 10.5 %copy-start.1 = (f32[64,2]{0,1:T(2,128)S(1)}, f32[64,2]{0,1:T(2,128)}, u32[]{:S(2)}) copy-start(f32[64,2]{0,1:T(2,128)} %param.11) | copy-start | bytes 1540
  24.3 10.5 %copy-start.2 = (s32[64,2]{0,1:T(2,128)S(1)}, s32[64,2]{0,1:T(2,128)}, u32[]{:S(2)}) copy-start(s32[64,2]{0,1:T(2,128)} %param.10) | copy-start | bytes 1540
  40.0 49.8 %copy-start = (f32[3072]{0:T(1024)S(1)}, f32[3072]{0:T(1024)}, u32[]{:S(2)}) copy-start(f32[3072]{0:T(1024)} %param.16) | copy-start | bytes 36868
  44.7 81.4 %all-reduce.6.cloned.1.call-start = ((), (), s32[]{:S(2)}) async-start(), calls=%async_computation.3 | async-start | bytes 1572864 | tf_op jit(solution)/shard_map/psum | solution.py:28
  89.8 64.9 %reduce-scatter.2.cloned.1.call-start = ((), (), s32[]{:S(2)}) async-start(), calls=%async_computation.4 | async-start | bytes 1572864 | tf_op jit(solution)/shard_map/reduce_scatter | solution.py:38
  89.9 66.0 %copy-start.3 = (s32[64]{0:T(128)S(1)}, s32[64]{0:T(128)}, u32[]{:S(2)}) copy-start(s32[64]{0:T(128)} %param.12) | copy-start | bytes 772
  133.0 11.7 %all-to-all-start = ((bf16[2,64,1536]{2,1,0:T(8,128)(2,1)}), bf16[2,64,1536]{2,1,0:T(8,128)(2,1)S(1)}, u32[]{:S(2)}, u32[]{:S(2)}) async-start(bf16[2,64,1536]{2,1,0:T(8,128)(2,1)} %bitcast.4), calls=%async_computation | async-start | bytes 786432 | tf_op jit(solution)/shard_map/all_to_all | solution.py:33
Sparse Core Ops, SparseCore 0:
  44.9 44.8 all-reduce.3
  92.1 33.9 all-reduce.5
  133.1 21.5 reduce-scatter.1
